TPU v7x, 256 devices: a whole 4x4x8 slice. The times are simulated.
256 devices in a mesh: expert: 64 (over x, z, core), dp: 4 (over y).
Axes of the slice: x: 4, y: 4, z: 8, core: 2. Of those that a mesh axis runs over, the one named last changes fastest.
Arguments:
- first_tokens: bfloat16 [16384, 7168], P(('dp', 'expert')), parts along dimension 0, may hold values from -6 to 6
- first_experts: int32 [16384, 1], P(('dp', 'expert')), parts along dimension 0, may hold values from 0 to 5
- first_replica: int32 [16384], P(('dp', 'expert')), parts along dimension 0, may hold values from 0 to 59
- first_gate: float32 [16384], P(('dp', 'expert')), parts along dimension 0, may hold values from 0.25 to 2.5
- second_tokens: bfloat16 [16384, 7168], P(('dp', 'expert')), parts along dimension 0, may hold values from -6 to 6
- second_experts: int32 [16384, 1], P(('dp', 'expert')), parts along dimension 0, may hold values from 0 to 5
- second_replica: int32 [16384], P(('dp', 'expert')), parts along dimension 0, may hold values from 0 to 59
- second_gate: float32 [16384], P(('dp', 'expert')), parts along dimension 0, may hold values from 0.25 to 2.5
- gate_weight: bfloat16 [229376, 1024], P(('dp', 'expert')), parts along dimension 0, may hold values from -0.0625 to 0.0625
- up_weight: bfloat16 [229376, 1024], P(('dp', 'expert')), parts along dimension 0, may hold values from -0.0625 to 0.0625
- down_weight: bfloat16 [229376, 1024], P(('dp', 'expert')), parts along dimension 0, may hold values from -0.1875 to 0.1875
- old_place: int32 [32], P('dp'), parts along dimension 0, may hold values from 0 to 5, as said below
- new_place: int32 [32], P('dp'), parts along dimension 0, may hold values from 0 to 5, as said below
- copy_source: int32 [32], P('dp'), parts along dimension 0, may hold values from 0 to 7, as said below
Outputs:
- first_out: bfloat16 [16384, 7168], P(('dp', 'expert')), parts along dimension 0
- second_out: bfloat16 [16384, 7168], P(('dp', 'expert')), parts along dimension 0
There are 4 independent parts, one for each index of `dp`. A program takes and returns all parts, laid end to end along the dimension named above; each array names one. Nothing has to cross between parts.
Inputs may be any that keep to these rules, and one draw needn't show every extreme that they name: `old_place`: every expert 0 to 5 is held by at least one slot. Every expert is held by at least one slot; new_place differs from old_place in at most 2 slots. old_place[copy_source[s]] == new_place[s] for every slot s, and copy_source[s] == s where new_place[s] == old_place[s].
All inputs are finite; a program needn't handle non-finite values.
Results may differ from a plain program's by a relative error of at most 0.0058.
Values may be sent and summed in bfloat16 or wider, within the bound.
No kernel may reach another device: no remote copies, remote signals or barrier semaphores. Data moves between devices by JAX's collectives and lax.ppermute only.
A program may use at most 256 MiB of HBM per device.

v0:
```python
import jax
import jax.numpy as jnp
from jax import lax
from jax.experimental import pallas as pl
from jax.experimental.pallas import tpu as pltpu
from jax.sharding import PartitionSpec as P

CAP = 12
LINE = 4
CORES = 2
MAIN = 32
SMALL = 16
MOST = 50
SERVED = 704
EMPTY = 64.0
LONG, LONGEST = 2 * EMPTY, 4 * EMPTY
SPOILT = 2.0**100
TILE = 256
EARLY, LATE = (3, 2), (1, 0)
ENDS, INNER = (0, 3), (1, 2)
LANES = 128
PARAMS = pltpu.CompilerParams(vmem_limit_bytes=60 * 1024 * 1024)


def ones_where(condition):
    return condition.astype(jnp.float32)


def exact(left, right):
    return jnp.dot(left.astype(jnp.bfloat16), right.astype(jnp.bfloat16), preferred_element_type=jnp.float32)


def iota(shape, dim):
    return lax.broadcasted_iota(jnp.int32, shape, dim)


def as_column(row):
    count = row.shape[1]
    same = iota((count, count), 0) == iota((count, count), 1)
    return jnp.sum(jnp.where(same, row, jnp.zeros((), row.dtype)), axis=1, keepdims=True)


def as_row(column, lanes, start):
    same = iota((column.shape[0], lanes), 0) + start == iota((column.shape[0], lanes), 1)
    return jnp.sum(jnp.where(same, column, jnp.zeros((), column.dtype)), axis=0, keepdims=True)


def routing(first_expert, second_expert, first_replica, second_replica, old_place, new_place, source):
    tokens, slots = first_expert.shape[1], source.shape[1]
    lanes = 2 * tokens
    expert = as_row(as_column(first_expert), lanes, 0) + as_row(as_column(second_expert), lanes, tokens)
    replica = as_row(as_column(first_replica), lanes, 0) + as_row(as_column(second_replica), lanes, tokens)
    replica = replica.astype(jnp.float32)
    lane = iota((1, lanes), 1)
    holds = jnp.where(lane < tokens, as_column(old_place), as_column(new_place))
    holder = ones_where(holds == expert)
    slot_row, slot_column = iota((slots, slots), 0), iota((slots, slots), 1)
    rank = exact(ones_where(slot_column < slot_row), holder)
    held_by = jnp.sum(holder, axis=0, keepdims=True)
    target = replica - held_by * jnp.floor((replica + 0.5) / held_by)
    picked = holder * ones_where(rank == target)
    earlier, later = iota((lanes, lanes), 0), iota((lanes, lanes), 1)
    before = earlier < later
    same_batch = (earlier < tokens) == (later < tokens)
    position = jnp.sum(exact(picked, ones_where(before & same_batch)) * picked, axis=0, keepdims=True)
    kept = picked * ones_where(position < CAP)
    taken = exact(ones_where(slot_row == source), kept)
    member = jnp.where(lane < tokens, kept, taken)
    place = jnp.sum(exact(member, ones_where(before)) * member, axis=0, keepdims=True)
    longest = jnp.max(jnp.sum(member, axis=1, keepdims=True), axis=0, keepdims=True)
    marked = ones_where(longest > MAIN)
    place = place + CORES * marked * ones_where(place >= MAIN - CORES)
    mark = EMPTY + (LONG - EMPTY) * marked + (LONGEST - LONG) * ones_where(longest > MAIN + SMALL - CORES)
    return member, place.astype(jnp.int32), mark


def agree(flags):
    parts = lax.axis_size("dp")
    others = [lax.ppermute(flags, "dp", [(i, (i + turn) % parts) for i in range(parts)]) for turn in range(1, parts)]
    for other in others:
        flags = jnp.maximum(flags, other)
    return flags


def table_of(member, place, start, rows, core):
    slots, tokens = member.shape
    row = iota((rows, tokens), 0)
    level = ones_where(place == start + CORES * row + (core + lax.axis_index("expert")) % CORES)
    return (member[:, None, :] * level[None, :, :]).reshape(slots * rows, tokens)


def fill(start, first_ref, second_ref, member, place, mark, out_ref):
    tokens = jnp.concatenate([first_ref[...], second_ref[...]], axis=0)
    slots, _, _, rows, width = out_ref.shape
    for core in range(CORES):
        table = table_of(member, place, start, rows, core)
        empty = mark * (1.0 - jnp.sum(table, axis=1, keepdims=True))
        packed = jnp.dot(table.astype(jnp.bfloat16), tokens, preferred_element_type=jnp.float32) + empty
        packed = packed.astype(jnp.bfloat16)
        if core == 1:
            packed = jnp.concatenate([packed[:, width // 2 :], packed[:, : width // 2]], axis=1)
        out_ref[:, 0, core] = packed.reshape(slots, rows, width)


def main_pack_kernel(first_ref, second_ref, *refs):
    inputs, (out_ref, member_ref, place_ref, mark_ref) = refs[:7], refs[7:]

    @pl.when(pl.program_id(0) == 0)
    def _():
        member_ref[...], place_ref[...], mark_ref[...] = routing(*[ref[...] for ref in inputs])

    fill(0, first_ref, second_ref, member_ref[...], place_ref[...], mark_ref[...], out_ref)


def later_pack_kernel(start, first_ref, second_ref, member_ref, place_ref, out_ref):
    fill(start, first_ref, second_ref, member_ref[...], place_ref[...], EMPTY, out_ref)


def whole(array):
    return pl.BlockSpec(array.shape, lambda n: (0,) * len(array.shape))


def pack(first_tokens, second_tokens, small, slots, start, places):
    tokens, width = first_tokens.shape[0], first_tokens.shape[1] // LINE
    rows = places // CORES
    token_spec = pl.BlockSpec((tokens, width), lambda j: (0, j))
    out_specs = [pl.BlockSpec((slots, 1, CORES, rows, width), lambda j: (0, j, 0, 0, 0))]
    out_shape = [jax.ShapeDtypeStruct((slots, LINE, CORES, rows, width), jnp.bfloat16)]
    if start is None:
        kernel = main_pack_kernel
        tables = [
            jax.ShapeDtypeStruct((slots, 2 * tokens), jnp.float32),
            jax.ShapeDtypeStruct((1, 2 * tokens), jnp.int32),
            jax.ShapeDtypeStruct((1, 1), jnp.float32),
        ]
        out_specs += [whole(table) for table in tables]
        out_shape += tables
    else:
        kernel = lambda *refs: later_pack_kernel(start, *refs)
    return pl.pallas_call(
        kernel,
        grid=(LINE,),
        in_specs=[token_spec, token_spec] + [whole(array) for array in small],
        out_specs=out_specs,
        out_shape=out_shape,
        compiler_params=PARAMS,
    )(first_tokens, second_tokens, *small)


def unpack_kernel(starts, member_ref, place_ref, first_gate_ref, second_gate_ref, *refs):
    first_ref, second_ref = refs[-2:]
    total = None
    for start, back_ref in zip(starts, refs[:-2]):
        slots, _, _, rows, width = back_ref.shape
        for core in range(CORES):
            table = table_of(member_ref[...], place_ref[...], start, rows, core).astype(jnp.bfloat16)
            back = back_ref[:, 0, core].reshape(slots * rows, width)
            if core == 1:
                back = jnp.concatenate([back[:, width // 2 :], back[:, : width // 2]], axis=1)
            part = lax.dot_general(table, back, (((0,), (0,)), ((), ())), preferred_element_type=jnp.float32)
            total = part if total is None else total + part
    tokens = first_ref.shape[0]
    first_ref[...] = (as_column(first_gate_ref[...]) * total[:tokens]).astype(first_ref.dtype)
    second_ref[...] = (as_column(second_gate_ref[...]) * total[tokens:]).astype(second_ref.dtype)


def unpack(first_gate, second_gate, member, place, starts, backs):
    tokens = first_gate.shape[0]
    line, width = backs[0].shape[1], backs[0].shape[4]
    out = jax.ShapeDtypeStruct((tokens, line * width), jnp.bfloat16)
    gate_spec = pl.BlockSpec((1, tokens), lambda j: (0, 0))
    back_specs = []
    for back in backs:
        slots, _, cores, rows, _ = back.shape
        back_specs.append(pl.BlockSpec((slots, 1, cores, rows, width), lambda j: (0, j, 0, 0, 0)))
    return pl.pallas_call(
        lambda *refs: unpack_kernel(starts, *refs),
        grid=(line,),
        in_specs=[
            pl.BlockSpec(member.shape, lambda j: (0, 0)),
            pl.BlockSpec(place.shape, lambda j: (0, 0)),
            gate_spec,
            gate_spec,
        ]
        + back_specs,
        out_specs=[pl.BlockSpec((tokens, width), lambda j: (0, j))] * 2,
        out_shape=[out, out],
        compiler_params=PARAMS,
    )(member, place, first_gate[None, :], second_gate[None, :], *backs)


def exchange(rows):
    return lax.all_to_all(rows, "expert", split_axis=0, concat_axis=0, tiled=True)


def across(value, apart, senders=range(LINE)):
    span = LINE * CORES
    pairs = []
    for device in range(lax.axis_size("expert")):
        if device % span // CORES in senders:
            pairs.append((device, device ^ (apart * CORES)))
    return lax.ppermute(value, "expert", pairs)


def numbering(rows_ref, served, share):
    received = rows_ref.shape[0]
    first = jnp.transpose(rows_ref[:, :LANES].astype(jnp.float32))[0:8, :]
    filled = ones_where(first < EMPTY / 2)
    within, group = iota((received, LANES), 0), iota((received, LANES), 1)
    inside = ones_where(within // share == group)
    totals = exact(filled, inside)
    ahead = exact(totals, ones_where(iota((LANES, LANES), 0) < iota((LANES, LANES), 1)))
    back_group, back_within = iota((LANES, received), 0), iota((LANES, received), 1)
    offset = exact_wide(ahead, ones_where(back_within // share == back_group))
    order = offset.astype(jnp.int32) + iota((8, received), 1) % share
    chunk = served // LINE
    quarter = sum((order >= chunk * k).astype(jnp.int32) for k in range(1, LINE))
    own = lax.axis_index("expert") // CORES % LINE
    order_here = order + ((quarter ^ own) - quarter) * chunk
    numbers = jnp.where((filled > 0.0) & (order < served), order_here, -1)
    marked = jnp.max(first, axis=1, keepdims=True)
    more = (marked > EMPTY).astype(jnp.int32) + (marked > LONG).astype(jnp.int32)
    overfull = (jnp.sum(filled, axis=1, keepdims=True) > served).astype(jnp.int32)
    return numbers, jnp.where(iota((8, LANES), 1) == 0, more, overfull)


def exact_wide(left, right):
    high = jnp.floor(left / 256.0)
    return 256.0 * exact(high, right) + exact(left - 256.0 * high, right)


def chunk_rows(target, rows_ref, packed_ref, chunks, chunk):
    received = rows_ref.shape[0]
    for place, k in enumerate(chunks):
        table = ones_where(iota((chunk, received), 0) + k * chunk == target[0:1, :]).astype(jnp.bfloat16)
        packed = jnp.dot(table, rows_ref[...], preferred_element_type=jnp.float32)
        packed_ref[place * chunk : (place + 1) * chunk, :] = packed.astype(jnp.bfloat16)


def multiply(packed_ref, weights, outs):
    half = packed_ref.shape[1] // 2
    sums = []
    for own_ref, other_ref in (weights[:2], weights[2:]):
        value = jnp.dot(packed_ref[:, :half], own_ref[...], preferred_element_type=jnp.float32)
        value += jnp.dot(packed_ref[:, half:], other_ref[...], preferred_element_type=jnp.float32)
        sums.append(value)
    both = jnp.concatenate(sums, axis=1)
    for place, out_ref in enumerate(outs):
        chunk = out_ref.shape[0]
        out_ref[...] = both[place * chunk : (place + 1) * chunk].astype(out_ref.dtype)


def early_kernel(served, share, rows_ref, *refs):
    weights, outs, (target_ref, flags_ref, packed_ref) = refs[:4], refs[4:-3], refs[-3:]

    @pl.when(pl.program_id(0) == 0)
    def _():
        target_ref[...], flags_ref[...] = numbering(rows_ref, served, share)
        chunk_rows(target_ref[...], rows_ref, packed_ref, EARLY, served // LINE)

    multiply(packed_ref, weights, outs)


def late_kernel(served, share, rows_ref, target_ref, *refs):
    weights, outs, (table_ref, packed_ref) = refs[:4], refs[4:-2], refs[-2:]

    @pl.when(pl.program_id(0) == 0)
    def _():
        chunk_rows(target_ref[...], rows_ref, packed_ref, LATE, served // LINE)
        column = jnp.transpose(target_ref[...].astype(jnp.float32))[:, 0:1].astype(jnp.int32)
        table_ref[...] = ones_where(iota(table_ref.shape, 1) == column).astype(jnp.bfloat16)

    multiply(packed_ref, weights, outs)


def partials(rows, target, served, share, in_w):
    (received, width), (depth, hidden) = rows.shape, in_w[0].shape
    chunk = served // LINE
    chunks = EARLY if target is None else LATE
    sums = [jax.ShapeDtypeStruct((chunk, 2 * hidden), jnp.bfloat16 if k else jnp.float32) for k in chunks]
    if target is None:
        kernel, small = early_kernel, []
        extra = [jax.ShapeDtypeStruct((8, received), jnp.int32), jax.ShapeDtypeStruct((8, LANES), jnp.int32)]
    else:
        kernel, small = late_kernel, [target]
        extra = [jax.ShapeDtypeStruct((received, served), jnp.bfloat16)]
    return pl.pallas_call(
        lambda *refs: kernel(served, share, *refs),
        grid=(hidden // TILE,),
        in_specs=[whole(rows)] + [whole(array) for array in small] + [pl.BlockSpec((depth, TILE), lambda n: (0, n))] * 4,
        out_specs=[pl.BlockSpec((chunk, 2 * TILE), lambda n: (0, n))] * len(chunks) + [whole(array) for array in extra],
        out_shape=sums + extra,
        scratch_shapes=[pltpu.VMEM((len(chunks) * chunk, width), jnp.bfloat16)],
        compiler_params=PARAMS,
    )(rows, *small, *in_w)


def add_kernel(*refs):
    total = refs[0][...].astype(jnp.float32)
    for other_ref in refs[1:-1]:
        total = total + other_ref[...].astype(jnp.float32)
    refs[-1][...] = total.astype(refs[-1].dtype)


def hidden_kernel(left_ref, right_ref, out_ref):
    total = left_ref[...] + right_ref[...].astype(jnp.float32)
    gate, up = total[:, :TILE], total[:, TILE:]
    out_ref[...] = (gate / (1.0 + jnp.exp(-gate)) * up).astype(jnp.bfloat16)


def by_tiles(kernel, arrays, tile, kind):
    chunk, double = arrays[0].shape
    tiles = double // (2 * TILE)
    return pl.pallas_call(
        kernel,
        grid=(tiles,),
        in_specs=[pl.BlockSpec((chunk, 2 * TILE), lambda n: (0, n))] * len(arrays),
        out_specs=pl.BlockSpec((chunk, tile), lambda n: (0, n)),
        out_shape=jax.ShapeDtypeStruct((chunk, tiles * tile), kind),
        compiler_params=PARAMS,
    )(*arrays)


def add(*arrays):
    return by_tiles(add_kernel, arrays, 2 * TILE, arrays[0].dtype)


def hidden_of(left, right):
    return by_tiles(hidden_kernel, (left, right), TILE, jnp.bfloat16)


def down_kernel(share, flags_ref, table_ref, *refs):
    chunks, (own_ref, other_ref, out_ref, wide_ref) = refs[: LINE + 1], refs[LINE + 1 :]

    @pl.when(pl.program_id(0) == 0)
    def _():
        parts = [chunk_ref[...] for chunk_ref in chunks]
        hidden = jnp.concatenate(parts[: LINE - 1] + [parts[LINE - 1] + parts[LINE]], axis=0)
        half = own_ref.shape[0]
        for place, weight_ref in enumerate((own_ref, other_ref)):
            out = lax.dot_general(hidden, weight_ref[...], (((1,), (1,)), ((), ())), preferred_element_type=jnp.float32)
            wide_ref[:, place * half : (place + 1) * half] = out.astype(jnp.bfloat16)

    spread = jnp.dot(table_ref[...], wide_ref[...], preferred_element_type=jnp.float32)
    spoilt = (flags_ref[0:1, 1:2] > 0) & (iota((spread.shape[0], 1), 0) % share == 0)
    out_ref[...] = jnp.where(spoilt, SPOILT, spread).astype(jnp.bfloat16)


def down(table, chunks, down_w, flags, share):
    received, served = table.shape
    width = 2 * down_w[0].shape[0]
    return pl.pallas_call(
        lambda *refs: down_kernel(share, *refs),
        grid=(received // TILE,),
        in_specs=[whole(flags), pl.BlockSpec((TILE, served), lambda m: (m, 0))]
        + [whole(chunk) for chunk in chunks]
        + [whole(weight) for weight in down_w],
        out_specs=pl.BlockSpec((TILE, width), lambda m: (m, 0)),
        out_shape=jax.ShapeDtypeStruct((received, width), jnp.bfloat16),
        scratch_shapes=[pltpu.VMEM((served, width), jnp.bfloat16)],
        compiler_params=PARAMS,
    )(flags, table, *chunks, *down_w)


def line_hidden(three, two, one, own, flags):
    inward = across(three, 1, ENDS)
    nearer = [across(three, 3, INNER), across(two, 2, ENDS), across(one, 1)]
    outward = across(add(two, inward), 2, INNER)
    if flags is not None:
        nearer, flags = lax.optimization_barrier((nearer, agree(flags)))
    return hidden_of(add(own, *nearer), outward), flags


def line_gather(hidden):
    one, two, three = across(hidden, 1), across(hidden, 2), across(hidden, 3, INNER)
    return [hidden, one, two, three, across(two, 1, INNER)]


def serve(spread, in_w, down_w, watched=False):
    blocks = (-1, *spread.shape[-2:])
    rows = exchange(spread.reshape(blocks))
    rows = rows.reshape(-1, rows.shape[-1])
    served, share = min(SERVED, rows.shape[0]), spread.shape[-2]
    three, two, target, flags = partials(rows, None, served, share, in_w)
    one, own, table = partials(rows, target, served, share, in_w)
    hidden, agreed = line_hidden(three, two, one, own, flags if watched else None)
    flags = agreed if watched else jnp.zeros_like(flags)
    out = down(table, line_gather(hidden), down_w, flags, share)
    return exchange(out.reshape(blocks)).reshape(spread.shape), flags


def swapped(weight):
    return lax.ppermute(weight, "expert", [(i, i ^ 1) for i in range(lax.axis_size("expert"))])


def per_device(
    first_tokens,
    first_experts,
    first_replica,
    first_gate,
    second_tokens,
    second_experts,
    second_replica,
    second_gate,
    gate_weight,
    up_weight,
    down_weight,
    old_place,
    new_place,
    copy_source,
):
    slots = copy_source.shape[0]
    raw = (first_experts, second_experts, first_replica, second_replica, old_place, new_place, copy_source)
    raw = [array.reshape(1, -1) for array in raw]
    spread, member, place, _ = pack(first_tokens, second_tokens, raw, slots, None, MAIN)
    in_w = (gate_weight, swapped(gate_weight), up_weight, swapped(up_weight))
    down_w = (down_weight, swapped(down_weight))
    main, flags = serve(spread, in_w, down_w, True)
    overfull = jnp.max(main[:, 0, :, 0, 0].astype(jnp.float32)) > SPOILT / 2
    crowd = jnp.where(overfull, 2, flags[0, 0])

    def batch(start, places):
        (rows,) = pack(first_tokens, second_tokens, [member, place], slots, start, places)
        return serve(rows, in_w, down_w)[0]

    def outputs(starts, backs):
        return tuple(unpack(first_gate, second_gate, member, place, starts, backs))

    def usual():
        return outputs([0], [main])

    def longer():
        return outputs([0, MAIN], [main, batch(MAIN, SMALL)])

    def fuller():
        starts = list(range(0, MOST, SMALL))
        return outputs(starts, [batch(start, SMALL) for start in starts])

    return lax.switch(crowd, [usual, longer, fuller])


def solution(mesh):
    placed = (
        P(("dp", "expert"), None),
        P(("dp", "expert"), None),
        P(("dp", "expert")),
        P(("dp", "expert")),
        P(("dp", "expert"), None),
        P(("dp", "expert"), None),
        P(("dp", "expert")),
        P(("dp", "expert")),
        P(("dp", "expert"), None),
        P(("dp", "expert"), None),
        P(("dp", "expert"), None),
        P("dp"),
        P("dp"),
        P("dp"),
    )
    return jax.shard_map(
        per_device,
        mesh=mesh,
        in_specs=placed,
        out_specs=(P(("dp", "expert"), None), P(("dp", "expert"), None)),
        check_vma=False,
    )
```

profile of v0, /device:TPU:1, one launch (start us, length us, event | category | flops | bytes accessed | tf_op | source)
XLA Modules:
  0.0 323.1 jit_solution(11114984878918758684)
XLA Ops:
  0.6 5.5 %shard_map.155 = (bf16[8,4,2,16,1792]{4,3,2,1,0:T(8,128)(2,1)}, f32[8,128]{1,0:T(8,128)S(1)}, s32[1,128]{1,0:T(1,128)S(1)}, f32[1,1]{1,0:T(1,128)}) custom-call(bf16[64,7168]{1,0:T(8,128)(2,1)} %first_ref.1, bf16[64,7168]{1,0:T(8,128)(2,1)} %second_ref.1, s32[1,64]{1,0:T(1,128)} %bitcast.60, s32[1,64]{1,0:T(1,128)} %bitcast.61, s32[1,64]{1,0:T(1,128)} %bitcast.62, ...), custom_call_target="tpu_custom_call" | custom-call | tf_op jit(solution)/shard_map/pallas_call | solution.py:140
  6.2 13.3 %all-to-all-start.10 = ((bf16[64,16,1792]{2,1,0:T(8,128)(2,1)}), bf16[64,16,1792]{2,1,0:T(8,128)(2,1)}, u32[]{:S(2)}, u32[]{:S(2)}) async-start(bf16[64,16,1792]{2,1,0:T(8,128)(2,1)} %bitcast.53), calls=%async_computation.10 | async-start | bytes 7340032 | tf_op jit(solution)/shard_map/all_to_all | solution.py:193
  19.5 0.6 collective-permute-start.45
  20.1 0.1 collective-permute-start.46
  20.2 4.9 %collective-permute-done.45.refs_2_.refs_3_ = bf16[896,1024]{1,0:T(8,128)(2,1)S(1)} collective-permute-done((bf16[896,1024]{1,0:T(8,128)(2,1)S(1)}, bf16[896,1024]{1,0:T(8,128)(2,1)S(1)}, u32[]{:S(2)}, u32[]{:S(2)}) %collective-permute-start.45) | collective-permute-done | bytes 1835040 | tf_op jit(solution)/shard_map/ppermute | solution.py:393
  25.1 1.2 copy-done.7
  26.3 0.1 collective-permute-done.46.refs_4_.refs_5_
  26.5 77.7 %all-to-all-done.10 = bf16[64,16,1792]{2,1,0:T(8,128)(2,1)} async-done(((bf16[64,16,1792]{2,1,0:T(8,128)(2,1)}), bf16[64,16,1792]{2,1,0:T(8,128)(2,1)}, u32[]{:S(2)}, u32[]{:S(2)}) %all-to-all-start.10) | async-done | bytes 3670048 | tf_op jit(solution)/shard_map/all_to_all | solution.py:193
  104.1 9.6 %shard_map.156 = (bf16[176,2048]{1,0:T(8,128)(2,1)}, bf16[176,2048]{1,0:T(8,128)(2,1)}, s32[8,1024]{1,0:T(8,128)}, s32[8,128]{1,0:T(8,128)}) custom-call(bf16[1024,1792]{1,0:T(8,128)(2,1)} %bitcast.34.refs_0_, bf16[896,1024]{1,0:T(8,128)(2,1)S(1)} %copy-done, bf16[896,1024]{1,0:T(8,128)(2,1)} %copy-done.7, bf16[896,1024]{1,0:T(8,128)(2,1)} %refs_4_.1, ...), custom_call_target="tpu_custom_call" | custom-call | tf_op jit(solution)/shard_map/pallas_call | solution.py:287
  113.8 3.1 collective-permute-start.53
  116.9 0.0 collective-permute-start.59
  116.9 2.7 collective-permute-start.52
  119.6 0.3 collective-permute-start.51
  120.0 0.7 collective-permute-start.50
  120.7 9.1 %shard_map.157 = (bf16[176,2048]{1,0:T(8,128)(2,1)}, f32[176,2048]{1,0:T(8,128)}, bf16[1024,704]{1,0:T(8,128)(2,1)}) custom-call(bf16[1024,1792]{1,0:T(8,128)(2,1)} %bitcast.34.refs_0_, s32[8,1024]{1,0:T(8,128)} %get-tuple-element.139.refs_1_, bf16[896,1024]{1,0:T(8,128)(2,1)S(1)} %copy-done, bf16[896,1024]{1,0:T(8,128)(2,1)} %copy-done.7, ...), custom_call_target="tpu_custom_call" | custom-call | tf_op jit(solution)/shard_map/pallas_call | solution.py:287
  129.8 0.0 collective-permute-done.52
  129.8 0.7 collective-permute-start.47
  130.5 0.9 collective-permute-start.49
  131.4 0.7 collective-permute-done.53.refs_1_
  132.1 2.9 collective-permute-start.48
  135.0 3.6 %shard_map.159 = bf16[176,2048]{1,0:T(8,128)(2,1)} custom-call(bf16[176,2048]{1,0:T(8,128)(2,1)} %get-tuple-element.138.refs_0_, bf16[176,2048]{1,0:T(8,128)(2,1)} %collective-permute-done.53.refs_1_), custom_call_target="tpu_custom_call" | custom-call | tf_op jit(solution)/shard_map/pallas_call | solution.py:314
  138.6 0.0 collective-permute-done.50
  138.6 1.3 collective-permute-start.54
  139.9 0.6 maximum_maximum_fusion.refs_0_
  140.5 7.1 %collective-permute-done.49.refs_3_ = bf16[176,2048]{1,0:T(8,128)(2,1)S(1)} collective-permute-done((bf16[176,2048]{1,0:T(8,128)(2,1)}, bf16[176,2048]{1,0:T(8,128)(2,1)S(1)}, u32[]{:S(2)}, u32[]{:S(2)}) %collective-permute-start.49) | collective-permute-done | bytes 720928 | tf_op jit(solution)/shard_map/ppermute | solution.py:202
  147.6 0.0 collective-permute-done.47.refs_1_
  147.6 13.8 %collective-permute-done.48.refs_2_ = bf16[176,2048]{1,0:T(8,128)(2,1)S(1)} collective-permute-done((bf16[176,2048]{1,0:T(8,128)(2,1)}, bf16[176,2048]{1,0:T(8,128)(2,1)S(1)}, u32[]{:S(2)}, u32[]{:S(2)}) %collective-permute-start.48) | collective-permute-done | bytes 720928 | tf_op jit(solution)/shard_map/ppermute | solution.py:202
  161.4 0.8 copy-done.17
  162.3 4.1 %shard_map.158.left_ref = f32[176,2048]{1,0:T(8,128)} custom-call(f32[176,2048]{1,0:T(8,128)} %get-tuple-element.144.refs_0_, bf16[176,2048]{1,0:T(8,128)(2,1)} %copy-done.15, bf16[176,2048]{1,0:T(8,128)(2,1)} %copy-done.17, bf16[176,2048]{1,0:T(8,128)(2,1)} %copy-done.16), custom_call_target="tpu_custom_call" | custom-call | tf_op jit(solution)/shard_map/pallas_call | solution.py:314
  166.4 11.3 %collective-permute-done.54.right_ref = bf16[176,2048]{1,0:T(8,128)(2,1)} collective-permute-done((bf16[176,2048]{1,0:T(8,128)(2,1)}, bf16[176,2048]{1,0:T(8,128)(2,1)}, u32[]{:S(2)}, u32[]{:S(2)}) %collective-permute-start.54) | collective-permute-done | bytes 720928 | tf_op jit(solution)/shard_map/ppermute | solution.py:202
  177.6 3.5 %shard_map.160.refs_2_ = bf16[176,1024]{1,0:T(8,128)(2,1)} custom-call(f32[176,2048]{1,0:T(8,128)} %shard_map.158.left_ref, bf16[176,2048]{1,0:T(8,128)(2,1)} %collective-permute-done.54.right_ref), custom_call_target="tpu_custom_call" | custom-call | tf_op jit(solution)/shard_map/pallas_call | solution.py:314
  181.2 0.0 collective-permute-start.56
  181.2 0.7 collective-permute-start.57
  181.8 4.1 %collective-permute-start.55 = (bf16[176,1024]{1,0:T(8,128)(2,1)}, bf16[176,1024]{1,0:T(8,128)(2,1)S(1)}, u32[]{:S(2)}, u32[]{:S(2)}) collective-permute-start(bf16[176,1024]{1,0:T(8,128)(2,1)} %shard_map.160.refs_2_), channel_id=1, source_target_pairs={{0,8},{4,12},{8,0},{12,4},{16,24},{20,28},{24,16},{28,20},{32,40},... | collective-permute-start | bytes 1081352 | tf_op jit(solution)/shard_map/ppermute | solution.py:202
  185.9 14.3 %collective-permute-done.56.refs_4_ = bf16[176,1024]{1,0:T(8,128)(2,1)S(1)} collective-permute-done((bf16[176,1024]{1,0:T(8,128)(2,1)}, bf16[176,1024]{1,0:T(8,128)(2,1)S(1)}, u32[]{:S(2)}, u32[]{:S(2)}) %collective-permute-start.56) | collective-permute-done | bytes 360480 | tf_op jit(solution)/shard_map/ppermute | solution.py:202
  200.2 1.3 collective-permute-start.58
  201.5 0.0 collective-permute-done.59.refs_8_
  201.5 0.0 collective-permute-done.55.refs_3_
  201.5 0.0 copy-start.32
  201.6 9.9 %collective-permute-done.58.refs_6_ = bf16[176,1024]{1,0:T(8,128)(2,1)S(1)} collective-permute-done((bf16[176,1024]{1,0:T(8,128)(2,1)S(1)}, bf16[176,1024]{1,0:T(8,128)(2,1)S(1)}, u32[]{:S(2)}, u32[]{:S(2)}) %collective-permute-start.58) | collective-permute-done | bytes 360480 | tf_op jit(solution)/shard_map/ppermute | solution.py:202
  211.5 0.7 copy-done.33
  212.2 10.4 %shard_map.161 = bf16[1024,1792]{1,0:T(8,128)(2,1)} custom-call(s32[8,128]{1,0:T(8,128)} %maximum_maximum_fusion.refs_0_, bf16[1024,704]{1,0:T(8,128)(2,1)} %get-tuple-element.143.refs_1_, bf16[176,1024]{1,0:T(8,128)(2,1)} %shard_map.160.refs_2_, bf16[176,1024]{1,0:T(8,128)(2,1)} %copy-done.32, bf16[176,1024]{1,0:T(8,128)(2,1)} %copy-done.30, ...), custom_call_target="tpu_custom_call" | custom-call | tf_op jit(solution)/shard_map/pallas_call | solution.py:352
  222.7 8.2 %all-to-all-start.11 = ((bf16[64,16,1792]{2,1,0:T(8,128)(2,1)}), bf16[64,16,1792]{2,1,0:T(8,128)(2,1)}, u32[]{:S(2)}, u32[]{:S(2)}) async-start(bf16[64,16,1792]{2,1,0:T(8,128)(2,1)} %bitcast.40), calls=%async_computation.11 | async-start | bytes 7340032 | tf_op jit(solution)/shard_map/all_to_all | solution.py:193
  230.9 1.2 slice.7
  232.1 83.5 %all-to-all-done.11 = bf16[64,16,1792]{2,1,0:T(8,128)(2,1)} async-done(((bf16[64,16,1792]{2,1,0:T(8,128)(2,1)}), bf16[64,16,1792]{2,1,0:T(8,128)(2,1)}, u32[]{:S(2)}, u32[]{:S(2)}) %all-to-all-start.11) | async-done | bytes 3670048 | tf_op jit(solution)/shard_map/all_to_all | solution.py:193
  315.5 1.4 slice_reduce_fusion
  318.3 4.8 %conditional.1 = ((bf16[64,7168]{1,0:T(8,128)(2,1)}, bf16[64,7168]{1,0:T(8,128)(2,1)})) conditional(s32[]{:T(128)} %clamp.3, (f32[64]{0:T(128)S(1)}, f32[64]{0:T(128)S(1)}, f32[8,128]{1,0:T(8,128)S(1)}, s32[1,128]{1,0:T(1,128)S(1)}, bf16[8,4,2,16,1792]{4,3,2,1,0:T(8,128)(2,1)}) %tuple.42, (f32[64]{0:T(128)S(1)}, f32[64]{0:T(128)S(1)}, ...), branch_computations={%region_1.2_spmd, %region_2.3_spmd, %region_3.4_spmd} | conditional | bytes 195303904 | solution.py:439
  318.3 4.8 %branch_0_fun.1 = (bf16[64,7168]{1,0:T(8,128)(2,1)}, bf16[64,7168]{1,0:T(8,128)(2,1)}) custom-call(f32[8,128]{1,0:T(8,128)S(1)} %get-tuple-element.60.refs_0_, s32[1,128]{1,0:T(1,128)S(1)} %get-tuple-element.61.refs_1_, f32[1,64]{1,0:T(1,128)S(1)} %bitcast.54, f32[1,64]{1,0:T(1,128)S(1)} %bitcast.57, bf16[8,4,2,16,1792]{4,3,2,1,0:T(8,128)(2,1)} %get-tuple-element.64.refs_4_), custom_call_target="tpu_custom_call" | custom-call | tf_op jit(solution)/shard_map/cond/branch_0_fun/pallas_call | solution.py:176
  (28 shorter events, 0.1 us)
Async XLA Ops:
  6.2 13.3 %copy-start = (bf16[896,1024]{1,0:T(8,128)(2,1)S(1)}, bf16[896,1024]{1,0:T(8,128)(2,1)}, u32[]{:S(2)}) copy-start(bf16[896,1024]{1,0:T(8,128)(2,1)} %refs_2_.1) | copy-start | bytes 5505028
  6.2 98.0 %all-to-all-start.10 = ((bf16[64,16,1792]{2,1,0:T(8,128)(2,1)}), bf16[64,16,1792]{2,1,0:T(8,128)(2,1)}, u32[]{:S(2)}, u32[]{:S(2)}) async-start(bf16[64,16,1792]{2,1,0:T(8,128)(2,1)} %bitcast.53), calls=%async_computation.10 | async-start | bytes 7340032 | tf_op jit(solution)/shard_map/all_to_all | solution.py:193
  19.5 5.6 %collective-permute-start.45 = (bf16[896,1024]{1,0:T(8,128)(2,1)S(1)}, bf16[896,1024]{1,0:T(8,128)(2,1)S(1)}, u32[]{:S(2)}, u32[]{:S(2)}) collective-permute-start(bf16[896,1024]{1,0:T(8,128)(2,1)S(1)} %copy-done), channel_id=1, source_target_pairs={{0,4},{4,0},{8,12},{12,8},{16,20},{20,16},{24,28},{28,24},{32,36},... | collective-permute-start | bytes 5505032 | tf_op jit(solution)/shard_map/ppermute | solution.py:393
  20.1 6.4 %collective-permute-start.46 = (bf16[896,1024]{1,0:T(8,128)(2,1)}, bf16[896,1024]{1,0:T(8,128)(2,1)}, u32[]{:S(2)}, u32[]{:S(2)}) collective-permute-start(bf16[896,1024]{1,0:T(8,128)(2,1)} %refs_4_.1), channel_id=1, source_target_pairs={{0,4},{4,0},{8,12},{12,8},{16,20},{20,16},{24,28},{28,24},{32,36},... | collective-permute-start | bytes 5505032 | tf_op jit(solution)/shard_map/ppermute | solution.py:393
  25.1 1.2 copy-start.7
  104.1 16.5 %copy-start.1 = (bf16[896,1024]{1,0:T(8,128)(2,1)S(1)}, bf16[896,1024]{1,0:T(8,128)(2,1)}, u32[]{:S(2)}) copy-start(bf16[896,1024]{1,0:T(8,128)(2,1)} %refs_4_.1) | copy-start | bytes 5505028
  113.8 18.3 %collective-permute-start.53 = (bf16[176,2048]{1,0:T(8,128)(2,1)}, bf16[176,2048]{1,0:T(8,128)(2,1)}, u32[]{:S(2)}, u32[]{:S(2)}) collective-permute-start(bf16[176,2048]{1,0:T(8,128)(2,1)} %get-tuple-element.137), channel_id=1, source_target_pairs={{0,8},{4,12},{24,16},{28,20},{32,40},{36,44},{56,48},{60,52},{64,7... | collective-permute-start | bytes 2162696 | tf_op jit(solution)/shard_map/ppermute | solution.py:202
  116.9 84.6 %collective-permute-start.59 = (bf16[896,1024]{1,0:T(8,128)(2,1)}, bf16[896,1024]{1,0:T(8,128)(2,1)}, u32[]{:S(2)}, u32[]{:S(2)}) collective-permute-start(bf16[896,1024]{1,0:T(8,128)(2,1)} %refs_7_.1), channel_id=1, source_target_pairs={{0,4},{4,0},{8,12},{12,8},{16,20},{20,16},{24,28},{28,24},{32,36},... | collective-permute-start | bytes 5505032 | tf_op jit(solution)/shard_map/ppermute | solution.py:393
  116.9 12.9 %collective-permute-start.52 = (s32[8,128]{1,0:T(8,128)}, s32[8,128]{1,0:T(8,128)S(1)}, u32[]{:S(2)}, u32[]{:S(2)}) collective-permute-start(s32[8,128]{1,0:T(8,128)} %get-tuple-element.141), channel_id=1, source_target_pairs={{0,3},{1,0},{2,1},{3,2},{4,7},{5,4},{6,5},{7,6},{8,11},{9,8},{10,9... | collective-permute-start | bytes 12296 | tf_op jit(solution)/shard_map/ppermute | solution.py:79
  119.6 10.9 %collective-permute-start.51 = (s32[8,128]{1,0:T(8,128)}, s32[8,128]{1,0:T(8,128)S(1)}, u32[]{:S(2)}, u32[]{:S(2)}) collective-permute-start(s32[8,128]{1,0:T(8,128)} %get-tuple-element.141), channel_id=1, source_target_pairs={{0,2},{1,3},{2,0},{3,1},{4,6},{5,7},{6,4},{7,5},{8,10},{9,11},{10,... | collective-permute-start | bytes 12296 | tf_op jit(solution)/shard_map/ppermute | solution.py:79
  120.0 18.6 %collective-permute-start.50 = (s32[8,128]{1,0:T(8,128)}, s32[8,128]{1,0:T(8,128)S(1)}, u32[]{:S(2)}, u32[]{:S(2)}) collective-permute-start(s32[8,128]{1,0:T(8,128)} %get-tuple-element.141), channel_id=1, source_target_pairs={{0,1},{1,2},{2,3},{3,0},{4,5},{5,6},{6,7},{7,4},{8,9},{9,10},{10,1... | collective-permute-start | bytes 12296 | tf_op jit(solution)/shard_map/ppermute | solution.py:79
  129.8 10.1 %copy-start.56 = (s32[8,128]{1,0:T(8,128)S(1)}, s32[8,128]{1,0:T(8,128)}, u32[]{:S(2)}) copy-start(s32[8,128]{1,0:T(8,128)} %get-tuple-element.141) | copy-start | bytes 12292
  129.8 17.8 %collective-permute-start.47 = (bf16[176,2048]{1,0:T(8,128)(2,1)}, bf16[176,2048]{1,0:T(8,128)(2,1)S(1)}, u32[]{:S(2)}, u32[]{:S(2)}) collective-permute-start(bf16[176,2048]{1,0:T(8,128)(2,1)} %get-tuple-element.137), channel_id=1, source_target_pairs={{8,16},{12,20},{16,8},{20,12},{40,48},{44,52},{48,40},{52,44},{72,... | collective-permute-start | bytes 2162696 | tf_op jit(solution)/shard_map/ppermute | solution.py:202
  130.5 17.1 %collective-permute-start.49 = (bf16[176,2048]{1,0:T(8,128)(2,1)}, bf16[176,2048]{1,0:T(8,128)(2,1)S(1)}, u32[]{:S(2)}, u32[]{:S(2)}) collective-permute-start(bf16[176,2048]{1,0:T(8,128)(2,1)} %get-tuple-element.140), channel_id=1, source_target_pairs={{0,8},{4,12},{8,0},{12,4},{16,24},{20,28},{24,16},{28,20},{32,40},... | collective-permute-start | bytes 2162696 | tf_op jit(solution)/shard_map/ppermute | solution.py:202
  132.1 29.3 %collective-permute-start.48 = (bf16[176,2048]{1,0:T(8,128)(2,1)}, bf16[176,2048]{1,0:T(8,128)(2,1)S(1)}, u32[]{:S(2)}, u32[]{:S(2)}) collective-permute-start(bf16[176,2048]{1,0:T(8,128)(2,1)} %get-tuple-element.138.refs_0_), channel_id=1, source_target_pairs={{0,16},{4,20},{24,8},{28,12},{32,48},{36,52},{56,40},{60,44},{64,8... | collective-permute-start | bytes 2162696 | tf_op jit(solution)/shard_map/ppermute | solution.py:202
  138.6 39.0 %collective-permute-start.54 = (bf16[176,2048]{1,0:T(8,128)(2,1)}, bf16[176,2048]{1,0:T(8,128)(2,1)}, u32[]{:S(2)}, u32[]{:S(2)}) collective-permute-start(bf16[176,2048]{1,0:T(8,128)(2,1)} %shard_map.159), channel_id=1, source_target_pairs={{8,24},{12,28},{16,0},{20,4},{40,56},{44,60},{48,32},{52,36},{72,8... | collective-permute-start | bytes 2162696 | tf_op jit(solution)/shard_map/ppermute | solution.py:202
  147.6 13.8 %copy-start.16 = (bf16[176,2048]{1,0:T(8,128)(2,1)}, bf16[176,2048]{1,0:T(8,128)(2,1)S(1)}, u32[]{:S(2)}) copy-start(bf16[176,2048]{1,0:T(8,128)(2,1)S(1)} %collective-permute-done.49.refs_3_) | copy-start | bytes 2162692
  147.6 13.8 %copy-start.15 = (bf16[176,2048]{1,0:T(8,128)(2,1)}, bf16[176,2048]{1,0:T(8,128)(2,1)S(1)}, u32[]{:S(2)}) copy-start(bf16[176,2048]{1,0:T(8,128)(2,1)S(1)} %collective-permute-done.47.refs_1_) | copy-start | bytes 2162692
  161.4 0.9 copy-start.17
  166.4 45.9 %copy-start.8 = (bf16[896,1024]{1,0:T(8,128)(2,1)S(1)}, bf16[896,1024]{1,0:T(8,128)(2,1)}, u32[]{:S(2)}) copy-start(bf16[896,1024]{1,0:T(8,128)(2,1)} %refs_7_.1) | copy-start | bytes 5505028
  181.2 19.0 %collective-permute-start.56 = (bf16[176,1024]{1,0:T(8,128)(2,1)}, bf16[176,1024]{1,0:T(8,128)(2,1)S(1)}, u32[]{:S(2)}, u32[]{:S(2)}) collective-permute-start(bf16[176,1024]{1,0:T(8,128)(2,1)} %shard_map.160.refs_2_), channel_id=1, source_target_pairs={{0,16},{4,20},{8,24},{12,28},{16,0},{20,4},{24,8},{28,12},{32,48},... | collective-permute-start | bytes 1081352 | tf_op jit(solution)/shard_map/ppermute | solution.py:202
  181.2 20.3 %collective-permute-start.57 = (bf16[176,1024]{1,0:T(8,128)(2,1)}, bf16[176,1024]{1,0:T(8,128)(2,1)S(1)}, u32[]{:S(2)}, u32[]{:S(2)}) collective-permute-start(bf16[176,1024]{1,0:T(8,128)(2,1)} %shard_map.160.refs_2_), channel_id=1, source_target_pairs={{8,16},{12,20},{16,8},{20,12},{40,48},{44,52},{48,40},{52,44},{72,... | collective-permute-start | bytes 1081352 | tf_op jit(solution)/shard_map/ppermute | solution.py:202
  181.8 19.7 %collective-permute-start.55 = (bf16[176,1024]{1,0:T(8,128)(2,1)}, bf16[176,1024]{1,0:T(8,128)(2,1)S(1)}, u32[]{:S(2)}, u32[]{:S(2)}) collective-permute-start(bf16[176,1024]{1,0:T(8,128)(2,1)} %shard_map.160.refs_2_), channel_id=1, source_target_pairs={{0,8},{4,12},{8,0},{12,4},{16,24},{20,28},{24,16},{28,20},{32,40},... | collective-permute-start | bytes 1081352 | tf_op jit(solution)/shard_map/ppermute | solution.py:202
  200.2 12.0 %copy-start.30 = (bf16[176,1024]{1,0:T(8,128)(2,1)}, bf16[176,1024]{1,0:T(8,128)(2,1)S(1)}, u32[]{:S(2)}) copy-start(bf16[176,1024]{1,0:T(8,128)(2,1)S(1)} %collective-permute-done.56.refs_4_) | copy-start | bytes 1081348
  200.2 11.3 %collective-permute-start.58 = (bf16[176,1024]{1,0:T(8,128)(2,1)S(1)}, bf16[176,1024]{1,0:T(8,128)(2,1)S(1)}, u32[]{:S(2)}, u32[]{:S(2)}) collective-permute-start(bf16[176,1024]{1,0:T(8,128)(2,1)S(1)} %collective-permute-done.56.refs_4_), channel_id=1, source_target_pairs={{8,0},{12,4},{16,24},{20,28},{40,32},{44,36},{48,56},{52,60},{72,6... | collective-permute-start | bytes 1081352 | tf_op jit(solution)/shard_map/ppermute | solution.py:202
  201.5 10.0 %copy-start.31 = (bf16[176,1024]{1,0:T(8,128)(2,1)}, bf16[176,1024]{1,0:T(8,128)(2,1)S(1)}, u32[]{:S(2)}) copy-start(bf16[176,1024]{1,0:T(8,128)(2,1)S(1)} %collective-permute-done.57.refs_5_) | copy-start | bytes 1081348
  201.5 9.9 %copy-start.32 = (bf16[176,1024]{1,0:T(8,128)(2,1)}, bf16[176,1024]{1,0:T(8,128)(2,1)S(1)}, u32[]{:S(2)}) copy-start(bf16[176,1024]{1,0:T(8,128)(2,1)S(1)} %collective-permute-done.55.refs_3_) | copy-start | bytes 1081348
  211.5 0.7 copy-start.33
  222.7 95.6 %copy-start.14 = (bf16[64,7168]{1,0:T(8,128)(2,1)S(1)}, bf16[64,7168]{1,0:T(8,128)(2,1)}, u32[]{:S(2)}) copy-start(bf16[64,7168]{1,0:T(8,128)(2,1)} %first_ref.1) | copy-start | bytes 2752516
  222.7 95.6 %copy-start.54 = (f32[64]{0:T(128)S(1)}, f32[64]{0:T(128)}, u32[]{:S(2)}) copy-start(f32[64]{0:T(128)} %param.20) | copy-start | bytes 772
  222.7 95.6 %copy-start.55 = (f32[64]{0:T(128)S(1)}, f32[64]{0:T(128)}, u32[]{:S(2)}) copy-start(f32[64]{0:T(128)} %param.24) | copy-start | bytes 772
  222.7 92.9 %all-to-all-start.11 = ((bf16[64,16,1792]{2,1,0:T(8,128)(2,1)}), bf16[64,16,1792]{2,1,0:T(8,128)(2,1)}, u32[]{:S(2)}, u32[]{:S(2)}) async-start(bf16[64,16,1792]{2,1,0:T(8,128)(2,1)} %bitcast.40), calls=%async_computation.11 | async-start | bytes 7340032 | tf_op jit(solution)/shard_map/all_to_all | solution.py:193
where the time goes:
time: 329 us; the launch traced here: 323 us
  waiting for transfers between devices  223 us (68%)
  Pallas kernels  50.7 us (15%)
  starting transfers between devices  40.9 us (12%)
  local copies, waits for them, and re-layouts  4.04 us (1%)
    all_to_all x2, waiting for transfers between devices, exchange(): lax.all_to_all(rows, 'expert', split_axis=0, concat_axis=0, tiled=True)  161 us
    ppermute x9, waiting for transfers between devices, across(): return lax.ppermute(value, 'expert', pairs)  57.1 us
    all_to_all x2, starting transfers between devices, exchange(): lax.all_to_all(rows, 'expert', split_axis=0, concat_axis=0, tiled=True)  21.5 us
    pallas_call x2, Pallas kernels, partials(): pl.pallas_call(lambda *refs: kernel(served, share, *refs), grid=(hidden /...  18.8 us
    ppermute x9, starting transfers between devices, across(): return lax.ppermute(value, 'expert', pairs)  14.9 us
    pallas_call x3, Pallas kernels, by_tiles(): pl.pallas_call(kernel, grid=(tiles,), in_specs=[pl.BlockSpec((chunk, 2 *...  11.2 us
    pallas_call x1, Pallas kernels, down(): pl.pallas_call(lambda *refs: down_kernel(share, *refs), grid=(received //...  10.4 us
  transfers between devices with their start and end apart: 17, of which 10 were waited for; matrix products, arithmetic and copies ran while one was open for 1% of the time, Pallas kernels for 6%

commit v1 on v0

--- a/solution.py
+++ b/solution.py
@@ -16,10 +16,12 @@
 LONG, LONGEST = 2 * EMPTY, 4 * EMPTY
 SPOILT = 2.0**100
 TILE = 256
-EARLY, LATE = (3, 2), (1, 0)
+EARLY, LATE = (3,), (2, 1, 0)
 ENDS, INNER = (0, 3), (1, 2)
 LANES = 128
+HINT = pl.CostEstimate(flops=1, bytes_accessed=1, transcendentals=0)
 PARAMS = pltpu.CompilerParams(vmem_limit_bytes=60 * 1024 * 1024)
+SMALLER = pltpu.CompilerParams(vmem_limit_bytes=24 * 1024 * 1024)
 
 
 def ones_where(condition):
@@ -230,11 +232,12 @@
 
 
 def chunk_rows(target, rows_ref, packed_ref, chunks, chunk):
-    received = rows_ref.shape[0]
-    for place, k in enumerate(chunks):
-        table = ones_where(iota((chunk, received), 0) + k * chunk == target[0:1, :]).astype(jnp.bfloat16)
-        packed = jnp.dot(table, rows_ref[...], preferred_element_type=jnp.float32)
-        packed_ref[place * chunk : (place + 1) * chunk, :] = packed.astype(jnp.bfloat16)
+    count, received = len(chunks) * chunk, rows_ref.shape[0]
+    row = iota((count, received), 0)
+    wanted = chunks[-1] * chunk + row
+    table = ones_where(wanted == target[0:1, :]).astype(jnp.bfloat16)
+    packed = jnp.dot(table, rows_ref[...], preferred_element_type=jnp.float32)
+    packed_ref[...] = packed.astype(jnp.bfloat16)
 
 
 def multiply(packed_ref, weights, outs):
@@ -245,7 +248,7 @@
         value += jnp.dot(packed_ref[:, half:], other_ref[...], preferred_element_type=jnp.float32)
         sums.append(value)
     both = jnp.concatenate(sums, axis=1)
-    for place, out_ref in enumerate(outs):
+    for place, out_ref in enumerate(reversed(outs)):
         chunk = out_ref.shape[0]
         out_ref[...] = both[place * chunk : (place + 1) * chunk].astype(out_ref.dtype)
 
@@ -262,13 +265,15 @@
 
 
 def late_kernel(served, share, rows_ref, target_ref, *refs):
-    weights, outs, (table_ref, packed_ref) = refs[:4], refs[4:-2], refs[-2:]
+    weights, outs, (table_ref, last_ref, packed_ref) = refs[:4], refs[4:-3], refs[-3:]
 
     @pl.when(pl.program_id(0) == 0)
     def _():
         chunk_rows(target_ref[...], rows_ref, packed_ref, LATE, served // LINE)
         column = jnp.transpose(target_ref[...].astype(jnp.float32))[:, 0:1].astype(jnp.int32)
         table_ref[...] = ones_where(iota(table_ref.shape, 1) == column).astype(jnp.bfloat16)
+        last = iota(last_ref.shape, 1) + table_ref.shape[1]
+        last_ref[...] = ones_where(last == column).astype(jnp.bfloat16)
 
     multiply(packed_ref, weights, outs)
 
@@ -283,7 +288,7 @@
         extra = [jax.ShapeDtypeStruct((8, received), jnp.int32), jax.ShapeDtypeStruct((8, LANES), jnp.int32)]
     else:
         kernel, small = late_kernel, [target]
-        extra = [jax.ShapeDtypeStruct((received, served), jnp.bfloat16)]
+        extra = [jax.ShapeDtypeStruct((received, count), jnp.bfloat16) for count in (served - chunk, chunk)]
     return pl.pallas_call(
         lambda *refs: kernel(served, share, *refs),
         grid=(hidden // TILE,),
@@ -292,6 +297,7 @@
         out_shape=sums + extra,
         scratch_shapes=[pltpu.VMEM((len(chunks) * chunk, width), jnp.bfloat16)],
         compiler_params=PARAMS,
+        cost_estimate=HINT,
     )(rows, *small, *in_w)
 
 
@@ -318,6 +324,7 @@
         out_specs=pl.BlockSpec((chunk, tile), lambda n: (0, n)),
         out_shape=jax.ShapeDtypeStruct((chunk, tiles * tile), kind),
         compiler_params=PARAMS,
+        cost_estimate=HINT,
     )(*arrays)
 
 
@@ -329,42 +336,61 @@
     return by_tiles(hidden_kernel, (left, right), TILE, jnp.bfloat16)
 
 
-def down_kernel(share, flags_ref, table_ref, *refs):
-    chunks, (own_ref, other_ref, out_ref, wide_ref) = refs[: LINE + 1], refs[LINE + 1 :]
+def widen(hidden, own_ref, other_ref, wide_ref):
+    half = own_ref.shape[0]
+    for place, weight_ref in enumerate((own_ref, other_ref)):
+        out = lax.dot_general(hidden, weight_ref[...], (((1,), (1,)), ((), ())), preferred_element_type=jnp.float32)
+        wide_ref[:, place * half : (place + 1) * half] = out.astype(jnp.bfloat16)
+
+
+def most_kernel(table_ref, *refs):
+    chunks, (own_ref, other_ref, out_ref, wide_ref) = refs[: LINE - 1], refs[LINE - 1 :]
 
     @pl.when(pl.program_id(0) == 0)
     def _():
-        parts = [chunk_ref[...] for chunk_ref in chunks]
-        hidden = jnp.concatenate(parts[: LINE - 1] + [parts[LINE - 1] + parts[LINE]], axis=0)
-        half = own_ref.shape[0]
-        for place, weight_ref in enumerate((own_ref, other_ref)):
-            out = lax.dot_general(hidden, weight_ref[...], (((1,), (1,)), ((), ())), preferred_element_type=jnp.float32)
-            wide_ref[:, place * half : (place + 1) * half] = out.astype(jnp.bfloat16)
+        widen(jnp.concatenate([chunk_ref[...] for chunk_ref in chunks], axis=0), own_ref, other_ref, wide_ref)
+
+    out_ref[...] = jnp.dot(table_ref[...], wide_ref[...], preferred_element_type=jnp.float32).astype(jnp.bfloat16)
+
+
+def last_kernel(share, flags_ref, most_ref, table_ref, left_ref, right_ref, own_ref, other_ref, out_ref, wide_ref):
+    @pl.when(pl.program_id(0) == 0)
+    def _():
+        widen(left_ref[...] + right_ref[...], own_ref, other_ref, wide_ref)
 
     spread = jnp.dot(table_ref[...], wide_ref[...], preferred_element_type=jnp.float32)
+    spread = spread + most_ref[...].astype(jnp.float32)
     spoilt = (flags_ref[0:1, 1:2] > 0) & (iota((spread.shape[0], 1), 0) % share == 0)
     out_ref[...] = jnp.where(spoilt, SPOILT, spread).astype(jnp.bfloat16)
 
 
-def down(table, chunks, down_w, flags, share):
-    received, served = table.shape
+def down(tables, chunks, down_w, flags, share):
+    received = tables[0].shape[0]
     width = 2 * down_w[0].shape[0]
-    return pl.pallas_call(
-        lambda *refs: down_kernel(share, *refs),
-        grid=(received // TILE,),
-        in_specs=[whole(flags), pl.BlockSpec((TILE, served), lambda m: (m, 0))]
-        + [whole(chunk) for chunk in chunks]
-        + [whole(weight) for weight in down_w],
-        out_specs=pl.BlockSpec((TILE, width), lambda m: (m, 0)),
-        out_shape=jax.ShapeDtypeStruct((received, width), jnp.bfloat16),
-        scratch_shapes=[pltpu.VMEM((served, width), jnp.bfloat16)],
-        compiler_params=PARAMS,
-    )(flags, table, *chunks, *down_w)
+
+    def call(kernel, count, *arrays, tiled):
+        return pl.pallas_call(
+            kernel,
+            grid=(received // TILE,),
+            in_specs=[
+                pl.BlockSpec((TILE, array.shape[1]), lambda m: (m, 0)) if place in tiled else whole(array)
+                for place, array in enumerate(arrays)
+            ],
+            out_specs=pl.BlockSpec((TILE, width), lambda m: (m, 0)),
+            out_shape=jax.ShapeDtypeStruct((received, width), jnp.bfloat16),
+            scratch_shapes=[pltpu.VMEM((count, width), jnp.bfloat16)],
+            compiler_params=SMALLER,
+            cost_estimate=HINT,
+        )(*arrays)
+
+    most = call(most_kernel, tables[0].shape[1], tables[0], *chunks[: LINE - 1], *down_w, tiled=(0,))
+    arrays = (flags, most, tables[1], *chunks[LINE - 1 :], *down_w)
+    return call(lambda *refs: last_kernel(share, *refs), tables[1].shape[1], *arrays, tiled=(1, 2))
 
 
 def line_hidden(three, two, one, own, flags):
-    inward = across(three, 1, ENDS)
-    nearer = [across(three, 3, INNER), across(two, 2, ENDS), across(one, 1)]
+    inward, inner = lax.optimization_barrier((across(three, 1, ENDS), across(three, 3, INNER)))
+    nearer = [inner, across(two, 2, ENDS), across(one, 1)]
     outward = across(add(two, inward), 2, INNER)
     if flags is not None:
         nearer, flags = lax.optimization_barrier((nearer, agree(flags)))
@@ -381,11 +407,11 @@
     rows = exchange(spread.reshape(blocks))
     rows = rows.reshape(-1, rows.shape[-1])
     served, share = min(SERVED, rows.shape[0]), spread.shape[-2]
-    three, two, target, flags = partials(rows, None, served, share, in_w)
-    one, own, table = partials(rows, target, served, share, in_w)
+    three, target, flags = partials(rows, None, served, share, in_w)
+    two, one, own, *tables = partials(rows, target, served, share, in_w)
     hidden, agreed = line_hidden(three, two, one, own, flags if watched else None)
     flags = agreed if watched else jnp.zeros_like(flags)
-    out = down(table, line_gather(hidden), down_w, flags, share)
+    out = down(tables, line_gather(hidden), down_w, flags, share)
     return exchange(out.reshape(blocks)).reshape(spread.shape), flags
 
 

time: 329 us -> 531 us (1.61)
  blocking collectives: 0 us -> 108 us
  Pallas kernels: 50.7 us -> 93 us
  starting transfers between devices: 40.9 us -> 60.2 us
  waiting for transfers between devices: 223 us -> 241 us
  loops' own time: 0.01 us -> 7.58 us
    all_to_all x0 -> x2, blocking collectives: none -> 108 us  [exchange(): lax.all_to_all(rows, 'expert', split_axis=0, concat_axis=0, tiled=True)]
    pallas_call x2 -> x4, Pallas kernels: 18.8 us -> 35.4 us  [partials(): pl.pallas_call(lambda *refs: kernel(served, share, *refs), grid=(hidden /...]
    ppermute x9 -> x18, starting transfers between devices: 14.9 us -> 29.7 us  [across(): return lax.ppermute(value, 'expert', pairs)]
    ppermute x9 -> x18, waiting for transfers between devices: 57.1 us -> 68 us  [across(): return lax.ppermute(value, 'expert', pairs)]
    pallas_call x3 -> x6, Pallas kernels: 11.2 us -> 22 us  [by_tiles(): pl.pallas_call(kernel, grid=(tiles,), in_specs=[pl.BlockSpec((chunk, 2 *...]
    pallas_call x1 -> x4, Pallas kernels: 10.4 us -> 20.3 us  [call(): pl.pallas_call(kernel, grid=(received // TILE,), in_specs=[pl.BlockSpec((...]
    another operation x1, loops' own time: 0.01 us -> 7.58 us  [per_device(): return lax.switch(crowd, [usual, longer, fuller])]
    ppermute x3, waiting for transfers between devices: 0.01 us -> 5.73 us  [agree(): lax.ppermute(flags, 'dp', [(i, (i + turn) % parts) for i in range(parts)])]
  transfers between devices with their start and end apart: 17 -> 26, of which waited for: 10 -> 17; matrix products, arithmetic and copies ran while one was open for 1% -> 0% of each run, Pallas kernels for 6% -> 10%
where the time goes in v1:
time: 531 us; the launch traced here: 521 us
  waiting for transfers between devices  241 us (45%)
  blocking collectives  108 us (20%)
  Pallas kernels  93 us (18%)
  starting transfers between devices  60.2 us (11%)
  loops' own time  7.58 us (1%)
  local copies, waits for them, and re-layouts  7.2 us (1%)
    all_to_all x2, waiting for transfers between devices, exchange(): lax.all_to_all(rows, 'expert', split_axis=0, concat_axis=0, tiled=True)  162 us
    all_to_all x2, blocking collectives, exchange(): lax.all_to_all(rows, 'expert', split_axis=0, concat_axis=0, tiled=True)  108 us
    ppermute x18, waiting for transfers between devices, across(): return lax.ppermute(value, 'expert', pairs)  68 us
    pallas_call x4, Pallas kernels, partials(): pl.pallas_call(lambda *refs: kernel(served, share, *refs), grid=(hidden /...  35.4 us
    ppermute x18, starting transfers between devices, across(): return lax.ppermute(value, 'expert', pairs)  29.7 us
    all_to_all x2, starting transfers between devices, exchange(): lax.all_to_all(rows, 'expert', split_axis=0, concat_axis=0, tiled=True)  22.2 us
    pallas_call x6, Pallas kernels, by_tiles(): pl.pallas_call(kernel, grid=(tiles,), in_specs=[pl.BlockSpec((chunk, 2 *...  22 us
    pallas_call x4, Pallas kernels, call(): pl.pallas_call(kernel, grid=(received // TILE,), in_specs=[pl.BlockSpec((...  20.3 us
  transfers between devices with their start and end apart: 26, of which 17 were waited for; matrix products, arithmetic and copies ran while one was open for 0% of the time, Pallas kernels for 10%

profile of v1, /device:TPU:1, one launch (start us, length us, event | category | flops | bytes accessed | tf_op | source)
XLA Modules:
  0.0 520.8 jit_solution(14352071297126072588)
XLA Ops:
  0.6 5.6 %shard_map.155 = (bf16[8,4,2,16,1792]{4,3,2,1,0:T(8,128)(2,1)}, f32[8,128]{1,0:T(8,128)S(1)}, s32[1,128]{1,0:T(1,128)S(1)}, f32[1,1]{1,0:T(1,128)}) custom-call(bf16[64,7168]{1,0:T(8,128)(2,1)} %first_ref.1, bf16[64,7168]{1,0:T(8,128)(2,1)} %second_ref.1, s32[1,64]{1,0:T(1,128)} %bitcast.57, s32[1,64]{1,0:T(1,128)} %bitcast.58, s32[1,64]{1,0:T(1,128)} %bitcast.59, ...), custom_call_target="tpu_custom_call" | custom-call | tf_op jit(solution)/shard_map/pallas_call | solution.py:142
  6.2 13.3 %all-to-all-start.10 = ((bf16[64,16,1792]{2,1,0:T(8,128)(2,1)}), bf16[64,16,1792]{2,1,0:T(8,128)(2,1)}, u32[]{:S(2)}, u32[]{:S(2)}) async-start(bf16[64,16,1792]{2,1,0:T(8,128)(2,1)} %bitcast.50), calls=%async_computation.10 | async-start | bytes 7340032 | tf_op jit(solution)/shard_map/all_to_all | solution.py:195
  20.2 4.9 collective-permute-done.45.refs_2_.refs_3_
  26.5 77.7 %all-to-all-done.10 = bf16[64,16,1792]{2,1,0:T(8,128)(2,1)} async-done(((bf16[64,16,1792]{2,1,0:T(8,128)(2,1)}), bf16[64,16,1792]{2,1,0:T(8,128)(2,1)}, u32[]{:S(2)}, u32[]{:S(2)}) %all-to-all-start.10) | async-done | bytes 3670048 | tf_op jit(solution)/shard_map/all_to_all | solution.py:195
  104.1 8.3 %shard_map.156 = (bf16[176,2048]{1,0:T(8,128)(2,1)}, s32[8,1024]{1,0:T(8,128)}, s32[8,128]{1,0:T(8,128)}) custom-call(bf16[1024,1792]{1,0:T(8,128)(2,1)} %bitcast.34.refs_0_, bf16[896,1024]{1,0:T(8,128)(2,1)} %refs_2_.1, bf16[896,1024]{1,0:T(8,128)(2,1)} %copy-done.25, bf16[896,1024]{1,0:T(8,128)(2,1)} %refs_4_.1, ...), custom_call_target="tpu_custom_call" | custom-call | flops 1 | bytes 1 | tf_op jit(solution)/shard_map/pallas_call | solution.py:292
  113.1 4.3 collective-permute-start.47
  117.4 1.6 collective-permute-start.57
  119.0 11.6 %shard_map.157 = (bf16[176,2048]{1,0:T(8,128)(2,1)}, bf16[176,2048]{1,0:T(8,128)(2,1)}, f32[176,2048]{1,0:T(8,128)}, bf16[1024,528]{1,0:T(8,128)(2,1)}, bf16[1024,176]{1,0:T(8,128)(2,1)}) custom-call(bf16[1024,1792]{1,0:T(8,128)(2,1)} %bitcast.34.refs_0_, s32[8,1024]{1,0:T(8,128)} %get-tuple-element.157.refs_1_, bf16[896,1024]{1,0:T(8,128)(2,1)} %refs_2_.1, ...), custom_call_target="tpu_custom_call" | custom-call | flops 1 | bytes 1 | tf_op jit(solution)/shard_map/pallas_call | solution.py:292
  130.6 4.0 collective-permute-start.49
  134.7 3.8 shard_map.159
  138.5 1.3 collective-permute-start.54
  139.8 2.8 collective-permute-start.53
  143.4 2.2 collective-permute-start.52
  145.5 1.8 collective-permute-done.52
  148.3 3.2 collective-permute-done.51
  151.5 4.3 collective-permute-done.50.refs_3_
  155.8 6.7 %collective-permute-done.49.refs_2_ = bf16[176,2048]{1,0:T(8,128)(2,1)} collective-permute-done((bf16[176,2048]{1,0:T(8,128)(2,1)}, bf16[176,2048]{1,0:T(8,128)(2,1)}, u32[]{:S(2)}, u32[]{:S(2)}) %collective-permute-start.49) | collective-permute-done | bytes 720928 | tf_op jit(solution)/shard_map/ppermute | solution.py:204
  162.5 4.1 shard_map.158.left_ref
  166.5 7.4 %collective-permute-done.54.right_ref = bf16[176,2048]{1,0:T(8,128)(2,1)} collective-permute-done((bf16[176,2048]{1,0:T(8,128)(2,1)}, bf16[176,2048]{1,0:T(8,128)(2,1)}, u32[]{:S(2)}, u32[]{:S(2)}) %collective-permute-start.54) | collective-permute-done | bytes 720928 | tf_op jit(solution)/shard_map/ppermute | solution.py:204
  173.9 3.5 shard_map.160.refs_0_
  177.5 2.9 collective-permute-start.55
  181.0 15.3 %collective-permute-done.56.refs_2_ = bf16[176,1024]{1,0:T(8,128)(2,1)S(1)} collective-permute-done((bf16[176,1024]{1,0:T(8,128)(2,1)}, bf16[176,1024]{1,0:T(8,128)(2,1)S(1)}, u32[]{:S(2)}, u32[]{:S(2)}) %collective-permute-start.56) | collective-permute-done | bytes 360480 | tf_op jit(solution)/shard_map/ppermute | solution.py:204
  196.3 1.5 collective-permute-start.59
  198.9 7.6 %shard_map.161.refs_1_ = bf16[1024,1792]{1,0:T(8,128)(2,1)S(1)} custom-call(bf16[1024,528]{1,0:T(8,128)(2,1)S(1)} %copy-done.2, bf16[176,1024]{1,0:T(8,128)(2,1)S(1)} %copy-done.1, bf16[176,1024]{1,0:T(8,128)(2,1)S(1)} %collective-permute-done.55.refs_1_, bf16[176,1024]{1,0:T(8,128)(2,1)S(1)} %collective-permute-done.56.refs_2_, ...), custom_call_target="tpu_custom_call" | custom-call | flops 1 | bytes 1 | tf_op jit(solution)/shard_map/pallas_call | solution.py:372
  206.9 4.4 shard_map.162
  211.4 1.9 copy-done
  213.3 9.0 %all-to-all-start.11 = ((bf16[64,16,1792]{2,1,0:T(8,128)(2,1)}), bf16[64,16,1792]{2,1,0:T(8,128)(2,1)}, u32[]{:S(2)}, u32[]{:S(2)}) async-start(bf16[64,16,1792]{2,1,0:T(8,128)(2,1)} %bitcast.38), calls=%async_computation.11 | async-start | bytes 7340032 | tf_op jit(solution)/shard_map/all_to_all | solution.py:195
  222.8 84.2 %all-to-all-done.11 = bf16[64,16,1792]{2,1,0:T(8,128)(2,1)} async-done(((bf16[64,16,1792]{2,1,0:T(8,128)(2,1)}), bf16[64,16,1792]{2,1,0:T(8,128)(2,1)}, u32[]{:S(2)}, u32[]{:S(2)}) %all-to-all-start.11) | async-done | bytes 3670048 | tf_op jit(solution)/shard_map/all_to_all | solution.py:195
  306.9 1.4 slice_reduce_fusion
  309.6 210.1 %conditional.1 = ((bf16[64,7168]{1,0:T(8,128)(2,1)}, bf16[64,7168]{1,0:T(8,128)(2,1)})) conditional(s32[]{:T(128)} %clamp.3, (f32[64]{0:T(128)S(1)}, f32[64]{0:T(128)S(1)}, f32[8,128]{1,0:T(8,128)S(1)}, s32[1,128]{1,0:T(1,128)S(1)}, bf16[8,4,2,16,1792]{4,3,2,1,0:T(8,128)(2,1)}) %tuple.49, (f32[64]{0:T(128)S(1)}, f32[64]{0:T(128)S(1)}, ...), branch_computations={%region_1.2_spmd, %region_2.3_spmd, %region_3.4_spmd} | conditional | flops 28 | bytes 182721024 | solution.py:465
  309.7 4.1 branch_1_fun.9
  313.8 51.3 %all_to_all.50 = bf16[64,8,1792]{2,1,0:T(8,128)(2,1)} all-to-all(bf16[64,8,1792]{2,1,0:T(8,128)(2,1)} %bitcast.48), channel_id=1, replica_groups=mesh['expert'=64,'dp'=4] {'expert'}, dimensions={0} | all-to-all | bytes 3670016 | tf_op jit(solution)/shard_map/cond/branch_1_fun/all_to_all | solution.py:195
  365.0 6.9 %branch_1_fun.10 = (bf16[128,2048]{1,0:T(8,128)(2,1)}, s32[8,512]{1,0:T(8,128)}, s32[8,128]{1,0:T(8,128)}) custom-call(bf16[512,1792]{1,0:T(8,128)(2,1)} %bitcast.41, bf16[896,1024]{1,0:T(8,128)(2,1)} %get-tuple-element.72.refs_1_.refs_2_, bf16[896,1024]{1,0:T(8,128)(2,1)} %get-tuple-element.73.refs_2_.refs_3_, ...), custom_call_target="tpu_custom_call" | custom-call | flops 1 | bytes 1 | tf_op jit(solution)/shard_map/cond/branch_1_fun/pallas_call | solution.py:292
  372.6 3.5 collective-permute-start
  376.1 8.7 %branch_1_fun.11 = (bf16[128,2048]{1,0:T(8,128)(2,1)}, bf16[128,2048]{1,0:T(8,128)(2,1)}, f32[128,2048]{1,0:T(8,128)}, bf16[512,384]{1,0:T(8,128)(2,1)}, bf16[512,128]{1,0:T(8,128)(2,1)}) custom-call(bf16[512,1792]{1,0:T(8,128)(2,1)} %bitcast.42, s32[8,512]{1,0:T(8,128)} %get-tuple-element.76.refs_1_, bf16[896,1024]{1,0:T(8,128)(2,1)} %get-tuple-element.72.refs_1_.refs_2_, ...), custom_call_target="tpu_custom_call" | custom-call | flops 1 | bytes 1 | tf_op jit(solution)/shard_map/cond/branch_1_fun/pallas_call | solution.py:292
  384.9 5.3 %collective-permute-start.2 = (bf16[128,2048]{1,0:T(8,128)(2,1)}, bf16[128,2048]{1,0:T(8,128)(2,1)}, u32[]{:S(2)}, u32[]{:S(2)}) collective-permute-start(bf16[128,2048]{1,0:T(8,128)(2,1)} %get-tuple-element.81.refs_0_), channel_id=1, source_target_pairs={{0,16},{4,20},{24,8},{28,12},{32,48},{36,52},{56,40},{60,44},{64,8... | collective-permute-start | bytes 1572872 | tf_op jit(solution)/shard_map/cond/branch_1_fun/ppermute | solution.py:204
  391.0 3.4 branch_1_fun.13
  394.4 1.3 collective-permute-start.4
  397.0 11.3 %collective-permute-done.2.refs_2_ = bf16[128,2048]{1,0:T(8,128)(2,1)} collective-permute-done((bf16[128,2048]{1,0:T(8,128)(2,1)}, bf16[128,2048]{1,0:T(8,128)(2,1)}, u32[]{:S(2)}, u32[]{:S(2)}) %collective-permute-start.2) | collective-permute-done | bytes 524320 | tf_op jit(solution)/shard_map/cond/branch_1_fun/ppermute | solution.py:204
  408.3 3.8 branch_1_fun.12.left_ref
  412.1 8.9 %collective-permute-done.4.right_ref = bf16[128,2048]{1,0:T(8,128)(2,1)S(1)} collective-permute-done((bf16[128,2048]{1,0:T(8,128)(2,1)}, bf16[128,2048]{1,0:T(8,128)(2,1)S(1)}, u32[]{:S(2)}, u32[]{:S(2)}) %collective-permute-start.4) | collective-permute-done | bytes 524320 | tf_op jit(solution)/shard_map/cond/branch_1_fun/ppermute | solution.py:204
  421.8 3.4 branch_1_fun.14.refs_0_
  426.9 11.4 %collective-permute-done.6.refs_2_ = bf16[128,1024]{1,0:T(8,128)(2,1)S(1)} collective-permute-done((bf16[128,1024]{1,0:T(8,128)(2,1)}, bf16[128,1024]{1,0:T(8,128)(2,1)S(1)}, u32[]{:S(2)}, u32[]{:S(2)}) %collective-permute-start.6) | collective-permute-done | bytes 262176 | tf_op jit(solution)/shard_map/cond/branch_1_fun/ppermute | solution.py:204
  438.3 1.7 collective-permute-start.8
  440.9 4.7 branch_1_fun.15.refs_1_
  446.7 3.6 branch_1_fun.16
  450.3 56.3 %all_to_all.51 = bf16[64,8,1792]{2,1,0:T(8,128)(2,1)} all-to-all(bf16[64,8,1792]{2,1,0:T(8,128)(2,1)S(1)} %bitcast.40), channel_id=1, replica_groups=mesh['expert'=64,'dp'=4] {'expert'}, dimensions={0} | all-to-all | bytes 3670016 | tf_op jit(solution)/shard_map/cond/branch_1_fun/all_to_all | solution.py:195
  506.6 5.7 %branch_1_fun.17 = (bf16[64,7168]{1,0:T(8,128)(2,1)}, bf16[64,7168]{1,0:T(8,128)(2,1)}) custom-call(f32[8,128]{1,0:T(8,128)S(1)} %get-tuple-element.65.refs_2_.refs_0_, s32[1,128]{1,0:T(1,128)S(1)} %get-tuple-element.66.refs_3_.refs_1_, f32[1,64]{1,0:T(1,128)S(1)} %bitcast.52, f32[1,64]{1,0:T(1,128)S(1)} %bitcast.55, ...), custom_call_target="tpu_custom_call" | custom-call | tf_op jit(solution)/shard_map/cond/branch_1_fun/pallas_call | solution.py:178
  (68 shorter events, 14.7 us)
Async XLA Ops:
  6.2 13.3 %copy-start.23 = (bf16[896,1024]{1,0:T(8,128)(2,1)S(1)}, bf16[896,1024]{1,0:T(8,128)(2,1)}, u32[]{:S(2)}) copy-start(bf16[896,1024]{1,0:T(8,128)(2,1)} %refs_2_.1) | copy-start | bytes 5505028
  6.2 98.0 %all-to-all-start.10 = ((bf16[64,16,1792]{2,1,0:T(8,128)(2,1)}), bf16[64,16,1792]{2,1,0:T(8,128)(2,1)}, u32[]{:S(2)}, u32[]{:S(2)}) async-start(bf16[64,16,1792]{2,1,0:T(8,128)(2,1)} %bitcast.50), calls=%async_computation.10 | async-start | bytes 7340032 | tf_op jit(solution)/shard_map/all_to_all | solution.py:195
  19.5 5.6 %collective-permute-start.45 = (bf16[896,1024]{1,0:T(8,128)(2,1)S(1)}, bf16[896,1024]{1,0:T(8,128)(2,1)S(1)}, u32[]{:S(2)}, u32[]{:S(2)}) collective-permute-start(bf16[896,1024]{1,0:T(8,128)(2,1)S(1)} %copy-done.23), channel_id=1, source_target_pairs={{0,4},{4,0},{8,12},{12,8},{16,20},{20,16},{24,28},{28,24},{32,36},... | collective-permute-start | bytes 5505032 | tf_op jit(solution)/shard_map/ppermute | solution.py:419
  20.1 6.4 %collective-permute-start.46 = (bf16[896,1024]{1,0:T(8,128)(2,1)}, bf16[896,1024]{1,0:T(8,128)(2,1)}, u32[]{:S(2)}, u32[]{:S(2)}) collective-permute-start(bf16[896,1024]{1,0:T(8,128)(2,1)} %refs_4_.1), channel_id=1, source_target_pairs={{0,4},{4,0},{8,12},{12,8},{16,20},{20,16},{24,28},{28,24},{32,36},... | collective-permute-start | bytes 5505032 | tf_op jit(solution)/shard_map/ppermute | solution.py:419
  25.1 1.2 copy-start.25
  104.1 13.3 %copy-start.19 = (bf16[896,1024]{1,0:T(8,128)(2,1)S(1)}, bf16[896,1024]{1,0:T(8,128)(2,1)}, u32[]{:S(2)}) copy-start(bf16[896,1024]{1,0:T(8,128)(2,1)} %refs_5_.1) | copy-start | bytes 5505028
  112.4 22.2 %collective-permute-start.48 = (bf16[176,2048]{1,0:T(8,128)(2,1)}, bf16[176,2048]{1,0:T(8,128)(2,1)S(1)}, u32[]{:S(2)}, u32[]{:S(2)}) collective-permute-start(bf16[176,2048]{1,0:T(8,128)(2,1)} %get-tuple-element.155), channel_id=1, source_target_pairs={{8,16},{12,20},{16,8},{20,12},{40,48},{44,52},{48,40},{52,44},{72,... | collective-permute-start | bytes 2162696 | tf_op jit(solution)/shard_map/ppermute | solution.py:204
  113.1 21.6 %collective-permute-start.47 = (bf16[176,2048]{1,0:T(8,128)(2,1)}, bf16[176,2048]{1,0:T(8,128)(2,1)}, u32[]{:S(2)}, u32[]{:S(2)}) collective-permute-start(bf16[176,2048]{1,0:T(8,128)(2,1)} %get-tuple-element.155), channel_id=1, source_target_pairs={{0,8},{4,12},{24,16},{28,20},{32,40},{36,44},{56,48},{60,52},{64,7... | collective-permute-start | bytes 2162696 | tf_op jit(solution)/shard_map/ppermute | solution.py:204
  117.4 80.4 %collective-permute-start.57 = (bf16[896,1024]{1,0:T(8,128)(2,1)S(1)}, bf16[896,1024]{1,0:T(8,128)(2,1)}, u32[]{:S(2)}, u32[]{:S(2)}) collective-permute-start(bf16[896,1024]{1,0:T(8,128)(2,1)S(1)} %copy-done.19), channel_id=1, source_target_pairs={{0,4},{4,0},{8,12},{12,8},{16,20},{20,16},{24,28},{28,24},{32,36},... | collective-permute-start | bytes 5505032 | tf_op jit(solution)/shard_map/ppermute | solution.py:419
  130.5 9.3 %copy-start.54 = (s32[8,128]{1,0:T(8,128)S(1)}, s32[8,128]{1,0:T(8,128)}, u32[]{:S(2)}) copy-start(s32[8,128]{1,0:T(8,128)} %get-tuple-element.160) | copy-start | bytes 12292
  130.5 25.2 %collective-permute-start.50 = (bf16[176,2048]{1,0:T(8,128)(2,1)}, bf16[176,2048]{1,0:T(8,128)(2,1)S(1)}, u32[]{:S(2)}, u32[]{:S(2)}) collective-permute-start(bf16[176,2048]{1,0:T(8,128)(2,1)} %get-tuple-element.159), channel_id=1, source_target_pairs={{0,8},{4,12},{8,0},{12,4},{16,24},{20,28},{24,16},{28,20},{32,40},... | collective-permute-start | bytes 2162696 | tf_op jit(solution)/shard_map/ppermute | solution.py:204
  130.6 31.8 %collective-permute-start.49 = (bf16[176,2048]{1,0:T(8,128)(2,1)}, bf16[176,2048]{1,0:T(8,128)(2,1)}, u32[]{:S(2)}, u32[]{:S(2)}) collective-permute-start(bf16[176,2048]{1,0:T(8,128)(2,1)} %get-tuple-element.158.refs_0_), channel_id=1, source_target_pairs={{0,16},{4,20},{24,8},{28,12},{32,48},{36,52},{56,40},{60,44},{64,8... | collective-permute-start | bytes 2162696 | tf_op jit(solution)/shard_map/ppermute | solution.py:204
  134.7 27.8 %copy-start.27 = (bf16[176,2048]{1,0:T(8,128)(2,1)}, bf16[176,2048]{1,0:T(8,128)(2,1)S(1)}, u32[]{:S(2)}) copy-start(bf16[176,2048]{1,0:T(8,128)(2,1)S(1)} %collective-permute-done.48.refs_1_) | copy-start | bytes 2162692
  138.5 35.4 %collective-permute-start.54 = (bf16[176,2048]{1,0:T(8,128)(2,1)}, bf16[176,2048]{1,0:T(8,128)(2,1)}, u32[]{:S(2)}, u32[]{:S(2)}) collective-permute-start(bf16[176,2048]{1,0:T(8,128)(2,1)} %shard_map.159), channel_id=1, source_target_pairs={{8,24},{12,28},{16,0},{20,4},{40,56},{44,60},{48,32},{52,36},{72,8... | collective-permute-start | bytes 2162696 | tf_op jit(solution)/shard_map/ppermute | solution.py:204
  139.8 3.6 collective-permute-start.53
  143.4 4.0 collective-permute-start.52
  147.3 4.2 collective-permute-start.51
  155.8 6.7 %copy-start.28 = (bf16[176,2048]{1,0:T(8,128)(2,1)}, bf16[176,2048]{1,0:T(8,128)(2,1)S(1)}, u32[]{:S(2)}) copy-start(bf16[176,2048]{1,0:T(8,128)(2,1)S(1)} %collective-permute-done.50.refs_3_) | copy-start | bytes 2162692
  166.5 31.3 %copy-start.2 = (bf16[1024,528]{1,0:T(8,128)(2,1)S(1)}, bf16[1024,528]{1,0:T(8,128)(2,1)}, u32[]{:S(2)}) copy-start(bf16[1024,528]{1,0:T(8,128)(2,1)} %get-tuple-element.162.table_ref) | copy-start | bytes 3244036
  177.5 18.9 %collective-permute-start.56 = (bf16[176,1024]{1,0:T(8,128)(2,1)}, bf16[176,1024]{1,0:T(8,128)(2,1)S(1)}, u32[]{:S(2)}, u32[]{:S(2)}) collective-permute-start(bf16[176,1024]{1,0:T(8,128)(2,1)} %shard_map.160.refs_0_), channel_id=1, source_target_pairs={{0,16},{4,20},{8,24},{12,28},{16,0},{20,4},{24,8},{28,12},{32,48},... | collective-permute-start | bytes 1081352 | tf_op jit(solution)/shard_map/ppermute | solution.py:204
  177.5 20.4 %collective-permute-start.55 = (bf16[176,1024]{1,0:T(8,128)(2,1)}, bf16[176,1024]{1,0:T(8,128)(2,1)S(1)}, u32[]{:S(2)}, u32[]{:S(2)}) collective-permute-start(bf16[176,1024]{1,0:T(8,128)(2,1)} %shard_map.160.refs_0_), channel_id=1, source_target_pairs={{0,8},{4,12},{8,0},{12,4},{16,24},{20,28},{24,16},{28,20},{32,40},... | collective-permute-start | bytes 1081352 | tf_op jit(solution)/shard_map/ppermute | solution.py:204
  180.4 26.1 %collective-permute-start.58 = (bf16[176,1024]{1,0:T(8,128)(2,1)}, bf16[176,1024]{1,0:T(8,128)(2,1)S(1)}, u32[]{:S(2)}, u32[]{:S(2)}) collective-permute-start(bf16[176,1024]{1,0:T(8,128)(2,1)} %shard_map.160.refs_0_), channel_id=1, source_target_pairs={{8,16},{12,20},{16,8},{20,12},{40,48},{44,52},{48,40},{52,44},{72,... | collective-permute-start | bytes 1081352 | tf_op jit(solution)/shard_map/ppermute | solution.py:204
  196.3 10.6 %collective-permute-start.59 = (bf16[176,1024]{1,0:T(8,128)(2,1)S(1)}, bf16[176,1024]{1,0:T(8,128)(2,1)S(1)}, u32[]{:S(2)}, u32[]{:S(2)}) collective-permute-start(bf16[176,1024]{1,0:T(8,128)(2,1)S(1)} %collective-permute-done.56.refs_2_), channel_id=1, source_target_pairs={{8,0},{12,4},{16,24},{20,28},{40,32},{44,36},{48,56},{52,60},{72,6... | collective-permute-start | bytes 1081352 | tf_op jit(solution)/shard_map/ppermute | solution.py:204
  197.9 1.0 copy-start.1
  198.9 8.0 %copy-start.8 = (bf16[1024,176]{1,0:T(8,128)(2,1)S(1)}, bf16[1024,176]{1,0:T(8,128)(2,1)}, u32[]{:S(2)}) copy-start(bf16[1024,176]{1,0:T(8,128)(2,1)} %get-tuple-element.168.refs_2_) | copy-start | bytes 1081348
  211.4 1.9 copy-start
  213.2 96.4 %copy-start.26 = (bf16[64,7168]{1,0:T(8,128)(2,1)S(1)}, bf16[64,7168]{1,0:T(8,128)(2,1)}, u32[]{:S(2)}) copy-start(bf16[64,7168]{1,0:T(8,128)(2,1)} %first_ref.1) | copy-start | bytes 2752516
  213.3 96.4 %copy-start.52 = (f32[64]{0:T(128)S(1)}, f32[64]{0:T(128)}, u32[]{:S(2)}) copy-start(f32[64]{0:T(128)} %param.20) | copy-start | bytes 772
  213.3 96.4 %copy-start.53 = (f32[64]{0:T(128)S(1)}, f32[64]{0:T(128)}, u32[]{:S(2)}) copy-start(f32[64]{0:T(128)} %param.24) | copy-start | bytes 772
  213.3 93.7 %all-to-all-start.11 = ((bf16[64,16,1792]{2,1,0:T(8,128)(2,1)}), bf16[64,16,1792]{2,1,0:T(8,128)(2,1)}, u32[]{:S(2)}, u32[]{:S(2)}) async-start(bf16[64,16,1792]{2,1,0:T(8,128)(2,1)} %bitcast.38), calls=%async_computation.11 | async-start | bytes 7340032 | tf_op jit(solution)/shard_map/all_to_all | solution.py:195
  371.9 18.3 %collective-permute-start.1 = (bf16[128,2048]{1,0:T(8,128)(2,1)}, bf16[128,2048]{1,0:T(8,128)(2,1)S(1)}, u32[]{:S(2)}, u32[]{:S(2)}) collective-permute-start(bf16[128,2048]{1,0:T(8,128)(2,1)} %get-tuple-element.79), channel_id=1, source_target_pairs={{8,16},{12,20},{16,8},{20,12},{40,48},{44,52},{48,40},{52,44},{72,... | collective-permute-start | bytes 1572872 | tf_op jit(solution)/shard_map/cond/branch_1_fun/ppermute | solution.py:204
  372.6 17.6 %collective-permute-start = (bf16[128,2048]{1,0:T(8,128)(2,1)}, bf16[128,2048]{1,0:T(8,128)(2,1)S(1)}, u32[]{:S(2)}, u32[]{:S(2)}) collective-permute-start(bf16[128,2048]{1,0:T(8,128)(2,1)} %get-tuple-element.79), channel_id=1, source_target_pairs={{0,8},{4,12},{24,16},{28,20},{32,40},{36,44},{56,48},{60,52},{64,7... | collective-permute-start | bytes 1572872 | tf_op jit(solution)/shard_map/cond/branch_1_fun/ppermute | solution.py:204
  384.8 12.2 %collective-permute-start.3 = (bf16[128,2048]{1,0:T(8,128)(2,1)}, bf16[128,2048]{1,0:T(8,128)(2,1)S(1)}, u32[]{:S(2)}, u32[]{:S(2)}) collective-permute-start(bf16[128,2048]{1,0:T(8,128)(2,1)} %get-tuple-element.82), channel_id=1, source_target_pairs={{0,8},{4,12},{8,0},{12,4},{16,24},{20,28},{24,16},{28,20},{32,40},... | collective-permute-start | bytes 1572872 | tf_op jit(solution)/shard_map/cond/branch_1_fun/ppermute | solution.py:204
  384.9 23.4 %collective-permute-start.2 = (bf16[128,2048]{1,0:T(8,128)(2,1)}, bf16[128,2048]{1,0:T(8,128)(2,1)}, u32[]{:S(2)}, u32[]{:S(2)}) collective-permute-start(bf16[128,2048]{1,0:T(8,128)(2,1)} %get-tuple-element.81.refs_0_), channel_id=1, source_target_pairs={{0,16},{4,20},{24,8},{28,12},{32,48},{36,52},{56,40},{60,44},{64,8... | collective-permute-start | bytes 1572872 | tf_op jit(solution)/shard_map/cond/branch_1_fun/ppermute | solution.py:204
  390.2 18.0 %copy-start.29 = (bf16[128,2048]{1,0:T(8,128)(2,1)}, bf16[128,2048]{1,0:T(8,128)(2,1)S(1)}, u32[]{:S(2)}) copy-start(bf16[128,2048]{1,0:T(8,128)(2,1)S(1)} %collective-permute-done.1.refs_1_) | copy-start | bytes 1572868 | tf_op jit(solution)/shard_map/cond
  390.2 0.8 copy-start.39
  394.4 26.6 %collective-permute-start.4 = (bf16[128,2048]{1,0:T(8,128)(2,1)}, bf16[128,2048]{1,0:T(8,128)(2,1)S(1)}, u32[]{:S(2)}, u32[]{:S(2)}) collective-permute-start(bf16[128,2048]{1,0:T(8,128)(2,1)} %branch_1_fun.13), channel_id=1, source_target_pairs={{8,24},{12,28},{16,0},{20,4},{40,56},{44,60},{48,32},{52,36},{72,8... | collective-permute-start | bytes 1572872 | tf_op jit(solution)/shard_map/cond/branch_1_fun/ppermute | solution.py:204
  397.0 11.3 %copy-start.34 = (bf16[128,2048]{1,0:T(8,128)(2,1)}, bf16[128,2048]{1,0:T(8,128)(2,1)S(1)}, u32[]{:S(2)}) copy-start(bf16[128,2048]{1,0:T(8,128)(2,1)S(1)} %collective-permute-done.3.refs_3_) | copy-start | bytes 1572868 | tf_op jit(solution)/shard_map/cond
  412.1 27.9 %copy-start.9 = (bf16[512,384]{1,0:T(8,128)(2,1)S(1)}, bf16[512,384]{1,0:T(8,128)(2,1)}, u32[]{:S(2)}) copy-start(bf16[512,384]{1,0:T(8,128)(2,1)} %get-tuple-element.77.table_ref) | copy-start | bytes 1179652 | tf_op jit(solution)/shard_map/cond
  421.0 0.8 copy-start.47
  425.2 13.1 %collective-permute-start.6 = (bf16[128,1024]{1,0:T(8,128)(2,1)}, bf16[128,1024]{1,0:T(8,128)(2,1)S(1)}, u32[]{:S(2)}, u32[]{:S(2)}) collective-permute-start(bf16[128,1024]{1,0:T(8,128)(2,1)} %branch_1_fun.14.refs_0_), channel_id=1, source_target_pairs={{0,16},{4,20},{8,24},{12,28},{16,0},{20,4},{24,8},{28,12},{32,48},... | collective-permute-start | bytes 786440 | tf_op jit(solution)/shard_map/cond/branch_1_fun/ppermute | solution.py:204
  425.2 14.8 %collective-permute-start.5 = (bf16[128,1024]{1,0:T(8,128)(2,1)}, bf16[128,1024]{1,0:T(8,128)(2,1)S(1)}, u32[]{:S(2)}, u32[]{:S(2)}) collective-permute-start(bf16[128,1024]{1,0:T(8,128)(2,1)} %branch_1_fun.14.refs_0_), channel_id=1, source_target_pairs={{0,8},{4,12},{8,0},{12,4},{16,24},{20,28},{24,16},{28,20},{32,40},... | collective-permute-start | bytes 786440 | tf_op jit(solution)/shard_map/cond/branch_1_fun/ppermute | solution.py:204
  426.2 19.4 %collective-permute-start.7 = (bf16[128,1024]{1,0:T(8,128)(2,1)}, bf16[128,1024]{1,0:T(8,128)(2,1)S(1)}, u32[]{:S(2)}, u32[]{:S(2)}) collective-permute-start(bf16[128,1024]{1,0:T(8,128)(2,1)} %branch_1_fun.14.refs_0_), channel_id=1, source_target_pairs={{8,16},{12,20},{16,8},{20,12},{40,48},{44,52},{48,40},{52,44},{72,... | collective-permute-start | bytes 786440 | tf_op jit(solution)/shard_map/cond/branch_1_fun/ppermute | solution.py:204
  438.3 8.4 %collective-permute-start.8 = (bf16[128,1024]{1,0:T(8,128)(2,1)S(1)}, bf16[128,1024]{1,0:T(8,128)(2,1)S(1)}, u32[]{:S(2)}, u32[]{:S(2)}) collective-permute-start(bf16[128,1024]{1,0:T(8,128)(2,1)S(1)} %collective-permute-done.6.refs_2_), channel_id=1, source_target_pairs={{8,0},{12,4},{16,24},{20,28},{40,32},{44,36},{48,56},{52,60},{72,6... | collective-permute-start | bytes 786440 | tf_op jit(solution)/shard_map/cond/branch_1_fun/ppermute | solution.py:204
  440.0 1.0 copy-start.3
  440.9 5.8 %copy-start.14 = (bf16[512,128]{1,0:T(8,128)(2,1)S(1)}, bf16[512,128]{1,0:T(8,128)(2,1)}, u32[]{:S(2)}) copy-start(bf16[512,128]{1,0:T(8,128)(2,1)} %get-tuple-element.86.refs_2_) | copy-start | bytes 393220 | tf_op jit(solution)/shard_map/cond
